TPU v7x, 128 devices: a whole 4x4x4 slice. The times are simulated.
128 devices in a mesh: basin: 16 (over x, y_lo, core), event: 8 (over z, y_hi).
Axes of the slice: x: 4, y: 4 (y_hi: 2, y_lo: 2; y = y_hi * 2 + y_lo), z: 4, core: 2. Of those that a mesh axis runs over, the one named last changes fastest.
Arguments:
- inputs: bfloat16 [8, 8, 6144, 256], P('event', None, 'basin'), may hold values from -6 to 6
- cotangent: bfloat16 [8, 6, 6144, 256], P('event', None, 'basin'), may hold values from -6 to 6
- conv_weight: bfloat16 [2, 256, 512], replicated, may hold values from -0.25 to 0.25
- conv_bias: float32 [512], replicated, may hold values from -4 to 4
- diffusion_weight: bfloat16 [5, 256, 256], replicated, may hold values from -0.15625 to 0.15625
- tiles_down: bfloat16 [48, 4, 128, 128], P('basin'), may hold values from -0.25 to 0.25
- tiles_up: bfloat16 [48, 4, 128, 128], P('basin'), may hold values from -0.25 to 0.25
- cols_down: int32 [48, 4], P('basin'), may hold values from 0 to 4, as said below
- cols_up: int32 [48, 4], P('basin'), may hold values from 0 to 4, as said below
- live_counts: int32 [16], P('basin'), may hold values from 192 to 384, as said below
Outputs:
- grad_inputs: bfloat16 [8, 8, 6144, 256], P('event', None, 'basin')
- grad_conv_weight: float32 [2, 256, 512], replicated
- grad_conv_bias: float32 [512], replicated
- grad_diffusion_weight: float32 [5, 256, 256], replicated
Inputs may be any that keep to these rules, and one draw needn't show every extreme that they name: `cols_down`: in every row block, slot 0 names the block before it and slot 1 the block after it; the other slots name a block at most one away. A value v names the partition's own block v - 1 of its 3; 0 names the last block of the partition before, and 4 the first block of the partition after. `cols_up`: as for cols_down. `live_counts`: some partition is full and some holds exactly 192 live reaches in every draw.
All inputs are finite; a program needn't handle non-finite values.
Results may differ from a plain program's by a relative error of at most 0.008.
Values may be sent and summed in bfloat16 or wider, within the bound.
A program may use at most 128 MiB of HBM per device.

v0:
```python
import functools

import jax
import jax.numpy as jnp
from jax import lax
from jax.experimental import pallas as pl
from jax.experimental.pallas import tpu as pltpu
from jax.sharding import PartitionSpec as P

MESH = pl.DeviceIdType.MESH
BF = jnp.bfloat16
F32 = jnp.float32
T_IN, T_OUT, STEP = 8, 6, 2
ROWS, CH, TILE, NB = 384, 256, 128, 3
EXT = ROWS + 4 * TILE
MATS = 10
GROUPS = (
    (0, 3, ("x", "z", "y")),
    (3, 3, ("z", "y", "x")),
    (6, 4, ("y", "x", "z")),
)


def dot(a, b):
    return jnp.dot(a, b, preferred_element_type=F32)


def place():
    b, e = lax.axis_index("basin"), lax.axis_index("event")
    pos = {"x": b // 4, "y": (e % 2) * 2 + (b // 2) % 2, "z": e // 2}
    return b, e, b % 2, pos


def peer(core, pos, axis, q):
    at = dict(pos)
    at[axis] = q
    x, y, z = at["x"], at["y"], at["z"]
    return ((x * 2 + y % 2) * 2 + core, z * 2 + y // 2)


def remote(src, dst, send, recv, to):
    return pltpu.make_async_remote_copy(
        src_ref=src, dst_ref=dst, send_sem=send, recv_sem=recv, device_id=to, device_id_type=MESH
    )


def rows_at(index, size):
    return pl.ds(pl.multiple_of(index * size, size), size)


def all_reduce(half_of, core, pos, sib, bufs, sems, beside):
    s0, r0, s1, whole, r1s, s2s, r2s, r3s, s4s = bufs
    c_send, c_recv, send, recv = sems
    for m in range(MATS):
        for c in range(2):
            s0[m, c] = half_of(m, c, 1 - core).astype(BF)
    first = remote(s0, r0, c_send.at[0], c_recv.at[0], sib)
    first.start()
    beside(0)
    first.wait()
    for m in range(MATS):
        for c in range(2):
            s1[m, c] = (half_of(m, c, core) + r0[m, c].astype(F32)).astype(BF)

    def exchange(stage, src_of, dst_of, in_of, axis_of):
        copies = []
        for g, (lo, n, axes) in enumerate(GROUPS):
            axis = axes[axis_of]
            a = pos[axis]
            for k in (1, 2, 3):
                q = (a + k) % 4
                args = (send.at[stage, g, k - 1], recv.at[stage, g, k - 1], peer(core, pos, axis, q))
                out = remote(src_of(g, q), dst_of(g, k, a), *args)
                out.start()
                back = remote(src_of(g, q), in_of(g, k, (a + 4 - k) % 4), *args)
                copies.append((g, out, back))
        return copies

    def finish(copies, g):
        for h, out, back in copies:
            if h == g:
                back.wait_recv()
                out.wait_send()

    r1_at = lambda g, k, a: r1s[g].at[k - 1]
    copies = exchange(
        0,
        lambda g, q: s1.at[GROUPS[g][0] : GROUPS[g][0] + GROUPS[g][1], :, rows_at(q, 32), :],
        r1_at,
        r1_at,
        0,
    )
    beside(1)
    for g, (lo, n, axes) in enumerate(GROUPS):
        finish(copies, g)
        total = s1[lo : lo + n, :, rows_at(pos[axes[0]], 32), :].astype(F32)
        for k in range(3):
            total = total + r1s[g][k].astype(F32)
        for half in range(2):
            for c in range(2):
                s2s[g][2 * half + c] = total[:, c, half * 16 : half * 16 + 16, :].astype(BF)
    r2_at = lambda g, k, a: r2s[g].at[k - 1]
    copies = exchange(1, lambda g, q: s2s[g].at[q], r2_at, r2_at, 1)
    beside(2)
    for g, (lo, n, axes) in enumerate(GROUPS):
        finish(copies, g)
        total = s2s[g][pos[axes[1]]].astype(F32)
        for k in range(3):
            total = total + r2s[g][k].astype(F32)
        r3s[g][pos[axes[2]]] = total.astype(BF)
    copies = exchange(
        2,
        lambda g, q: r3s[g].at[pos[GROUPS[g][2][2]]],
        lambda g, k, a: r3s[g].at[a],
        lambda g, k, a: r3s[g].at[a],
        2,
    )
    beside(3)

    def spot(g, a):
        lo, n, axes = GROUPS[g]
        row = pl.ds(pl.multiple_of(pos[axes[0]] * 32 + (a // 2) * 16, 16), 16)
        return whole.at[core, lo : lo + n, a % 2, row, :]

    for g, (lo, n, axes) in enumerate(GROUPS):
        finish(copies, g)
        total = r3s[g][0].astype(F32)
        for k in range(1, 4):
            total = total + r3s[g][k].astype(F32)
        a = pos[axes[1]]
        row = pl.ds(pl.multiple_of(pos[axes[0]] * 32 + (a // 2) * 16, 16), 16)
        whole[core, lo : lo + n, a % 2, row, :] = total.astype(BF)
    copies = exchange(
        3,
        lambda g, q: spot(g, pos[GROUPS[g][2][1]]),
        lambda g, k, a: spot(g, a),
        lambda g, k, a: spot(g, a),
        1,
    )
    beside(4)

    def band(g, a):
        lo, n, axes = GROUPS[g]
        return whole.at[core, lo : lo + n, :, rows_at(a, 32), :]

    for g in range(len(GROUPS)):
        finish(copies, g)
    copies = exchange(
        4,
        lambda g, q: band(g, pos[GROUPS[g][2][0]]),
        lambda g, k, a: band(g, a),
        lambda g, k, a: band(g, a),
        0,
    )
    beside(5)
    last = []
    for g, (lo, n, axes) in enumerate(GROUPS):
        finish(copies, g)
        args = (c_send.at[1 + g], c_recv.at[1 + g], sib)
        out = remote(whole.at[core, lo : lo + n], whole.at[core, lo : lo + n], *args)
        out.start()
        last.append((out, remote(whole.at[core, lo : lo + n], whole.at[1 - core, lo : lo + n], *args)))
    beside(6)
    for out, back in last:
        back.wait_recv()
        out.wait_send()


def ar_scratch():
    n = len(GROUPS)
    bufs = [
        pltpu.VMEM((MATS, 2, TILE, TILE), BF),
        pltpu.VMEM((MATS, 2, TILE, TILE), BF),
        pltpu.VMEM((MATS, 2, TILE, TILE), BF),
        pltpu.VMEM((2, MATS, 2, TILE, TILE), BF),
    ]
    bufs += [pltpu.VMEM((3, g[1], 2, 32, TILE), BF) for g in GROUPS]
    bufs += [pltpu.VMEM((4, g[1], 16, TILE), BF) for g in GROUPS]
    bufs += [pltpu.VMEM((3, g[1], 16, TILE), BF) for g in GROUPS]
    bufs += [pltpu.VMEM((4, g[1], 16, TILE), BF) for g in GROUPS]
    sems = [
        pltpu.SemaphoreType.DMA((1 + n,)),
        pltpu.SemaphoreType.DMA((1 + n,)),
        pltpu.SemaphoreType.DMA((5, n, 3)),
        pltpu.SemaphoreType.DMA((5, n, 3)),
    ]
    return bufs, sems


def split_ar(refs):
    n = len(GROUPS)
    bufs = (*refs[:4], refs[4 : 4 + n], refs[4 + n : 4 + 2 * n], refs[4 + 2 * n : 4 + 3 * n], refs[4 + 3 * n : 4 + 4 * n], None)
    return bufs, refs[4 + 4 * n :]


def body(
    scale, x_in, cot_in, cw_in, cb_in, dw_in, td_in, tu_in, cd_in, cu_in, live_in,
    gi_out, gc_out, gb_out, gd_out,
    xs, cext, cw, cb, dw, tiles, vown, send_l, send_r, recv_l, recv_r, big, mask,
    wcat, cwt, ht, xt, ab, feats, gps, gacc, cacc, bacc,
    load_sem, tile_send, tile_recv, halo_send, halo_recv, *ar_refs,
):
    b, e, core, pos = place()
    right, left = ((b + 1) % 16, e), ((b + 15) % 16, e)
    sib = (b + 1 - 2 * core, e)
    barrier = pltpu.get_barrier_semaphore()
    greeted = [left, right] + [
        peer(core, pos, axis, (pos[axis] + k) % 4) for axis in ("x", "y", "z") for k in (1, 2, 3)
    ]
    for to in greeted:
        pl.semaphore_signal(barrier, inc=1, device_id=to, device_id_type=MESH)
    loads = [
        pltpu.make_async_copy(src, dst, load_sem.at[i])
        for i, (src, dst) in enumerate(
            [
                (td_in, tiles.at[0]),
                (tu_in, tiles.at[1]),
                (x_in, xs),
                (cw_in, cw),
                (cb_in, cb),
                (cot_in, cext.at[:, 2 * TILE : 2 * TILE + ROWS, :]),
                (dw_in, dw),
            ]
        )
    ]
    for load in loads:
        load.start()

    live = live_in[0]
    reach = lax.broadcasted_iota(jnp.int32, (ROWS, CH), 0)
    mask[...] = jnp.where((reach < live - TILE) | (reach >= ROWS - TILE), 1.0, 0.0).astype(F32)
    loads[0].wait()
    loads[1].wait()
    for way, cols in enumerate((cd_in, cu_in)):
        for r in range(NB):
            keep = mask[r * TILE : (r + 1) * TILE, :TILE]
            slots = [tiles[way, r, k].astype(F32) for k in range(4)]
            for o in range(3):
                total = jnp.zeros((TILE, TILE), F32)
                if o == 0:
                    total = total + slots[0]
                if o == 2:
                    total = total + slots[1]
                for k in (2, 3):
                    total = total + jnp.where(cols[r, k] - r == o, 1.0, 0.0).astype(F32) * slots[k]
                total = total * keep
                if r == 0 and o == 0:
                    total = total * jnp.where(b > 0, 1.0, 0.0).astype(F32)
                if r == NB - 1 and o == 2:
                    total = total * jnp.where(b < 15, 1.0, 0.0).astype(F32)
                tile = total.T.astype(BF)
                vown[way, r, o] = tile
                if (r, o) in ((1, 2), (2, 1), (2, 2)):
                    send_r[way, ((1, 2), (2, 1), (2, 2)).index((r, o))] = tile
                if (r, o) in ((0, 0), (0, 1), (1, 0)):
                    send_l[way, ((0, 0), (0, 1), (1, 0)).index((r, o))] = tile

    pl.semaphore_wait(barrier, len(greeted))
    tile_copies = [
        remote(send_r, recv_l, tile_send.at[0], tile_recv.at[0], right),
        remote(send_l, recv_r, tile_send.at[1], tile_recv.at[1], left),
    ]
    for copy in tile_copies:
        copy.start()

    def halo(t):
        return [
            remote(
                cot_in.at[t, TILE:ROWS, :], cext.at[t, 0 : 2 * TILE, :],
                halo_send.at[t, 0], halo_recv.at[t, 0], right,
            ),
            remote(
                cot_in.at[t, 0 : 2 * TILE, :], cext.at[t, 2 * TILE + ROWS : EXT, :],
                halo_send.at[t, 1], halo_recv.at[t, 1], left,
            ),
        ]

    @pl.loop(0, T_OUT)
    def _(t):
        for copy in halo(t):
            copy.start()

    for load in loads[2:]:
        load.wait()

    @pl.loop(0, T_OUT)
    def _(t):
        pre = dot(xs[t], cw[0]) + dot(xs[t + STEP], cw[1]) + cb[...]
        f = jnp.tanh(pre[:, :CH])
        s = 0.5 * jnp.tanh(0.5 * pre[:, CH:]) + 0.5
        sm = s * mask[...]
        fs = f * sm
        ht[t] = fs.astype(BF).T
        ab[t, :, :CH] = sm * (1.0 - f * f)
        ab[t, :, CH:] = fs * (1.0 - s)

    @pl.loop(0, T_IN)
    def _(t):
        xt[t] = xs[t].T

    for k in range(5):
        wcat[k * CH : (k + 1) * CH, :] = dw[k].T
    for k in range(2):
        cwt[k] = cw[k].T
    gps[0:STEP] = jnp.zeros((STEP, ROWS, 2 * CH), BF)
    gacc[...] = jnp.zeros_like(gacc)
    cacc[...] = jnp.zeros_like(cacc)
    bacc[...] = jnp.zeros_like(bacc)

    for copy in tile_copies:
        copy.wait()

    def v(way, i, k):
        if 0 <= i < NB:
            return vown[way, i, k - i + 1]
        if i < 0:
            return recv_l[way, ((-2, -1), (-1, -1), (-1, 0)).index((i, k))]
        return recv_r[way, ((3, 2), (3, 3), (4, 3)).index((i, k))]

    for j in range(NB):
        for way in range(2):
            for at, i in enumerate(range(j - 2, j + 3)):
                total = jnp.zeros((TILE, TILE), F32)
                for k in range(j - 1, j + 2):
                    if abs(i - k) <= 1:
                        total = total + dot(v(way, k, j), v(way, i, k))
                first = v(way, i, j) if abs(i - j) <= 1 else jnp.zeros((TILE, TILE), BF)
                big[j, way * TILE : (way + 1) * TILE, at * TILE : (at + 1) * TILE] = first
                big[j, (2 + way) * TILE : (3 + way) * TILE, at * TILE : (at + 1) * TILE] = total.astype(BF)

    @pl.loop(0, T_OUT)
    def _(t):
        for copy in halo(t):
            copy.wait()
        feats[:, :CH] = cext[t, 2 * TILE : 2 * TILE + ROWS, :]
        for j in range(NB):
            out = dot(big[j], cext[t, j * TILE : (j + 5) * TILE, :]).astype(BF)
            for at, k in enumerate((1, 3, 2, 4)):
                feats[j * TILE : (j + 1) * TILE, k * CH : (k + 1) * CH] = out[at * TILE : (at + 1) * TILE]
        gacc[...] += dot(ht[t], feats[...])
        gh = dot(feats[...], wcat[...])
        ga = gh * ab[t, :, :CH]
        gb = gh * ab[t, :, CH:]
        gp = jnp.concatenate([ga, gb], axis=1).astype(BF)
        gps[t + STEP] = gp
        cacc[0] += dot(xt[t], gp)
        cacc[1] += dot(xt[t + STEP], gp)
        bacc[...] += jnp.sum(gp.astype(F32).reshape(ROWS // 8, 8, 2 * CH), axis=0)
        before = jnp.maximum(t - STEP, 0)
        own = cext[before, 2 * TILE : 2 * TILE + ROWS, :].astype(F32) * mask[...]
        own = own * jnp.where(t >= STEP, 1.0, 0.0).astype(F32)
        gi_out[t] = (dot(gp, cwt[0]) + dot(gps[t], cwt[1]) + own).astype(BF)

    line = jnp.sum(bacc[...], axis=0, keepdims=True)
    row = lax.broadcasted_iota(jnp.int32, (16, TILE), 0)
    bias = jnp.zeros((16, TILE), F32)
    for i in range(4):
        bias = bias + jnp.where(row == i, jnp.broadcast_to(line[:, i * TILE : (i + 1) * TILE], (16, TILE)), 0.0)
    bias = jnp.broadcast_to(bias[None], (TILE // 16, 16, TILE)).reshape(TILE, TILE)

    def half_of(m, c, half):
        if m < 5:
            return gacc[rows_at(half, TILE), m * CH + c * TILE : m * CH + (c + 1) * TILE]
        if m < 9:
            at = ((m - 5) % 2) * CH + c * TILE
            return cacc[(m - 5) // 2, rows_at(half, TILE), at : at + TILE]
        return bias

    def beside(stage):
        if stage < STEP:
            t = T_OUT + stage
            own = cext[t - STEP, 2 * TILE : 2 * TILE + ROWS, :].astype(F32) * mask[...]
            gi_out[t] = (dot(gps[t], cwt[1]) + own).astype(BF)

    bufs, sems = split_ar(ar_refs)
    all_reduce(half_of, core, pos, sib, bufs, sems, beside)
    whole = bufs[3]
    for h in range(2):
        for c in range(2):
            rows = slice(h * TILE, (h + 1) * TILE)
            for m in range(9):
                part = whole[h, m, c].astype(F32) * scale
                if m < 5:
                    gd_out[m, rows, c * TILE : (c + 1) * TILE] = part
                else:
                    at = ((m - 5) % 2) * CH + c * TILE
                    gc_out[(m - 5) // 2, rows, at : at + TILE] = part
    gb_out[...] = whole[0, 9, 0, 0:16, :].astype(F32) * scale


def on_device(x, cot, cw, cb, dw, td, tu, cd, cu, live):
    scale = float(8 * T_OUT * 6144) ** (-0.5)
    bufs, sems = ar_scratch()
    anywhere = pl.BlockSpec(memory_space=pl.ANY)
    vmem = pl.BlockSpec(memory_space=pltpu.VMEM)
    smem = pl.BlockSpec(memory_space=pltpu.SMEM)
    gi, gc, gb, gd = pl.pallas_call(
        functools.partial(body, scale),
        out_shape=(
            jax.ShapeDtypeStruct((T_IN, ROWS, CH), BF),
            jax.ShapeDtypeStruct((2, CH, 2 * CH), F32),
            jax.ShapeDtypeStruct((16, TILE), F32),
            jax.ShapeDtypeStruct((5, CH, CH), F32),
        ),
        in_specs=[anywhere] * 7 + [smem] * 3,
        out_specs=(vmem,) * 4,
        scratch_shapes=[
            pltpu.VMEM((T_IN, ROWS, CH), BF),
            pltpu.VMEM((T_OUT, EXT, CH), BF),
            pltpu.VMEM((2, CH, 2 * CH), BF),
            pltpu.VMEM((1, 2 * CH), F32),
            pltpu.VMEM((5, CH, CH), BF),
            pltpu.VMEM((2, NB, 4, TILE, TILE), BF),
            pltpu.VMEM((2, NB, 3, TILE, TILE), BF),
            pltpu.VMEM((2, 3, TILE, TILE), BF),
            pltpu.VMEM((2, 3, TILE, TILE), BF),
            pltpu.VMEM((2, 3, TILE, TILE), BF),
            pltpu.VMEM((2, 3, TILE, TILE), BF),
            pltpu.VMEM((NB, 4 * TILE, 5 * TILE), BF),
            pltpu.VMEM((ROWS, CH), F32),
            pltpu.VMEM((5 * CH, CH), BF),
            pltpu.VMEM((2, 2 * CH, CH), BF),
            pltpu.VMEM((T_OUT, CH, ROWS), BF),
            pltpu.VMEM((T_IN, CH, ROWS), BF),
            pltpu.VMEM((T_OUT, ROWS, 2 * CH), F32),
            pltpu.VMEM((ROWS, 5 * CH), BF),
            pltpu.VMEM((T_IN, ROWS, 2 * CH), BF),
            pltpu.VMEM((CH, 5 * CH), F32),
            pltpu.VMEM((2, CH, 2 * CH), F32),
            pltpu.VMEM((8, 2 * CH), F32),
            pltpu.SemaphoreType.DMA((7,)),
            pltpu.SemaphoreType.DMA((2,)),
            pltpu.SemaphoreType.DMA((2,)),
            pltpu.SemaphoreType.DMA((T_OUT, 2)),
            pltpu.SemaphoreType.DMA((T_OUT, 2)),
            *bufs,
            *sems,
        ],
        compiler_params=pltpu.CompilerParams(
            collective_id=0, has_side_effects=True, vmem_limit_bytes=56 << 20
        ),
    )(x[0], cot[0], cw, cb.reshape(1, -1), dw, td, tu, cd, cu, live)
    return gi[None], gc, gb[0:4].reshape(-1), gd


def solution(mesh):
    return jax.shard_map(
        on_device,
        mesh=mesh,
        in_specs=(
            P("event", None, "basin", None),
            P("event", None, "basin", None),
            P(),
            P(),
            P(),
            P("basin", None, None, None),
            P("basin", None, None, None),
            P("basin", None),
            P("basin", None),
            P("basin"),
        ),
        out_specs=(P("event", None, "basin", None), P(), P(), P()),
        check_vma=False,
    )
```

profile of v0, /device:TPU:1, one launch (start us, length us, event | category | flops | bytes accessed | tf_op | source)
XLA Modules:
  0.0 73.9 jit_solution(1863546788376812090)
XLA Ops:
  1.3 65.8 %shard_map.129 = (bf16[8,384,256]{2,1,0:T(8,128)(2,1)}, f32[2,256,512]{2,1,0:T(8,128)}, f32[16,128]{1,0:T(8,128)}, f32[5,256,256]{2,1,0:T(8,128)}) custom-call(bf16[8,384,256]{2,1,0:T(8,128)(2,1)} %bitcast.7, bf16[6,384,256]{2,1,0:T(8,128)(2,1)} %bitcast.8, bf16[2,256,512]{2,1,0:T(8,128)(2,1)} %cw_in.1, f32[1,512]{1,0:T(1,128)} %bitcast.9, ...), custom_call_target="tpu_custom_call" | custom-call | tf_op jit(solution)/shard_map/pallas_call | solution.py:397
  67.1 1.3 %slice_bitcast_fusion = f32[512]{0:T(512)} fusion(f32[16,128]{1,0:T(8,128)} %get-tuple-element.10), kind=kLoop, calls=%fused_computation | loop fusion | bytes 4096 | tf_op jit(solution)/shard_map/reshape | solution.py:443
  68.4 0.0 copy-start.1
  68.4 2.7 %copy.18 = bf16[1,8,384,256]{3,2,1,0:T(8,128)(2,1)} copy(bf16[1,8,384,256]{3,2,1,0:T(8,128)(2,1)} %bitcast.6) | data formatting | bytes 3145728
  71.1 0.0 copy-done.1
  71.1 0.0 copy-start
  71.1 1.0 %copy.19 = f32[2,256,512]{2,1,0:T(8,128)} copy(f32[2,256,512]{2,1,0:T(8,128)S(1)} %copy-done.1) | data formatting | bytes 2097152
  72.1 0.7 copy-done
  72.8 1.1 %copy.20 = f32[5,256,256]{2,1,0:T(8,128)} copy(f32[5,256,256]{2,1,0:T(8,128)S(1)} %copy-done) | data formatting | bytes 2621440
Async XLA Ops:
  68.4 2.7 %copy-start.1 = (f32[2,256,512]{2,1,0:T(8,128)S(1)}, f32[2,256,512]{2,1,0:T(8,128)}, u32[]{:S(2)}) copy-start(f32[2,256,512]{2,1,0:T(8,128)} %get-tuple-element.17) | copy-start | bytes 3145732
  71.1 1.7 %copy-start = (f32[5,256,256]{2,1,0:T(8,128)S(1)}, f32[5,256,256]{2,1,0:T(8,128)}, u32[]{:S(2)}) copy-start(f32[5,256,256]{2,1,0:T(8,128)} %get-tuple-element.19) | copy-start | bytes 3932164
where the time goes:
time: 74.1 us; the launch traced here: 73.9 us
  Pallas kernels  65.8 us (89%)
  local copies, waits for them, and re-layouts  6.75 us (9%)
  between operations  1.29 us (2%)
    pallas_call x1, Pallas kernels, on_device(): pl.pallas_call(functools.partial(body, scale), out_shape=(jax.ShapeDtypeS...  65.8 us
    unnamed x7, local copies, waits for them, and re-layouts  5.49 us

commit v1 on v0

v1 whole, which is shorter than its diff:
```python
import functools

import jax
import jax.numpy as jnp
from jax import lax
from jax.experimental import pallas as pl
from jax.experimental.pallas import tpu as pltpu
from jax.sharding import PartitionSpec as P

MESH = pl.DeviceIdType.MESH
BF = jnp.bfloat16
F32 = jnp.float32
T_IN, T_OUT, STEP = 8, 6, 2
ROWS, CH, TILE, NB = 384, 256, 128, 3
EXT = ROWS + 4 * TILE
MATS = 10
GROUPS = (
    (0, 3, ("x", "z", "y")),
    (3, 3, ("z", "y", "x")),
    (6, 4, ("y", "x", "z")),
)


def dot(a, b):
    return jnp.dot(a, b, preferred_element_type=F32)


def place():
    b, e = lax.axis_index("basin"), lax.axis_index("event")
    pos = {"x": b // 4, "y": (e % 2) * 2 + (b // 2) % 2, "z": e // 2}
    return b, e, b % 2, pos


def peer(core, pos, moved):
    x, y, z = ({**pos, **moved}[axis] for axis in ("x", "y", "z"))
    return ((x * 2 + y % 2) * 2 + core, z * 2 + y // 2)


def remote(src, dst, send, recv, to):
    return pltpu.make_async_remote_copy(
        src_ref=src, dst_ref=dst, send_sem=send, recv_sem=recv, device_id=to, device_id_type=MESH
    )


def rows_at(index, size):
    return pl.ds(pl.multiple_of(index * size, size), size)


class AllReduce:
    def __init__(self, half_of, core, pos, sib, bufs, sems):
        self.half_of, self.core, self.pos, self.sib = half_of, core, pos, sib
        self.s0, self.r0, self.s1, self.whole, self.r1s, self.s2s, self.r2s, self.r3s = bufs
        self.c_send, self.c_recv, self.send, self.recv = sems
        self.flying = {}

    def core_send(self, g):
        lo, n, _ = GROUPS[g]
        for m in range(lo, lo + n):
            for c in range(2):
                self.s0[m, c] = self.half_of(m, c, 1 - self.core).astype(BF)
        mats = pl.ds(lo, n)
        copy = remote(self.s0.at[mats], self.r0.at[mats], self.c_send.at[0, g], self.c_recv.at[0, g], self.sib)
        copy.start()
        self.flying["core", g] = copy

    def exchange(self, stage, g, src_of, dst_of, in_of, axis):
        a = self.pos[axis]
        copies = []
        for k in (1, 2, 3):
            q = (a + k) % 4
            args = (self.send.at[stage, g, k - 1], self.recv.at[stage, g, k - 1], peer(self.core, self.pos, {axis: q}))
            out = remote(src_of(q), dst_of(k, a), *args)
            out.start()
            copies.append((out, remote(src_of(q), in_of(k, (a + 4 - k) % 4), *args)))
        self.flying[stage, g] = copies

    def finish(self, stage, g):
        for out, back in self.flying[stage, g]:
            back.wait_recv()

    def scatter_first(self, g):
        lo, n, axes = GROUPS[g]
        self.flying["core", g].wait()
        for m in range(lo, lo + n):
            for c in range(2):
                self.s1[m, c] = (self.half_of(m, c, self.core) + self.r0[m, c].astype(F32)).astype(BF)
        dst = lambda k, a: self.r1s[g].at[k - 1]
        self.exchange(0, g, lambda q: self.s1.at[lo : lo + n, :, rows_at(q, 32), :], dst, dst, axes[0])

    def scatter_second(self, g):
        lo, n, axes = GROUPS[g]
        self.finish(0, g)
        total = self.s1[lo : lo + n, :, rows_at(self.pos[axes[0]], 32), :].astype(F32)
        for k in range(3):
            total = total + self.r1s[g][k].astype(F32)
        for half in range(2):
            for c in range(2):
                self.s2s[g][2 * half + c] = total[:, c, half * 16 : half * 16 + 16, :]
        dst = lambda k, a: self.r2s[g].at[k - 1]
        self.exchange(1, g, lambda q: self.s2s[g].at[q], dst, dst, axes[1])

    def sum_third(self, g):
        lo, n, axes = GROUPS[g]
        self.finish(1, g)
        total = self.s2s[g][self.pos[axes[1]]]
        for k in range(3):
            total = total + self.r2s[g][k]
        a = self.pos[axes[2]]
        self.r3s[g][a] = total
        dst = lambda k, a: self.r3s[g].at[a]
        self.exchange(2, g, lambda q: self.r3s[g].at[a], dst, dst, axes[2])

    def spot(self, g, a):
        lo, n, axes = GROUPS[g]
        row = pl.ds(pl.multiple_of(self.pos[axes[0]] * 32 + (a // 2) * 16, 16), 16)
        return self.core, pl.ds(lo, n), a % 2, row, slice(None)

    def gather_second(self, g):
        lo, n, axes = GROUPS[g]
        self.finish(2, g)
        total = self.r3s[g][0]
        for k in range(1, 4):
            total = total + self.r3s[g][k]
        a = self.pos[axes[1]]
        self.whole[self.spot(g, a)] = total.astype(BF)
        dst = lambda k, a: self.whole.at[self.spot(g, a)]
        self.exchange(3, g, lambda q: self.whole.at[self.spot(g, a)], dst, dst, axes[1])

    def band(self, g, a, core):
        lo, n, axes = GROUPS[g]
        return self.whole.at[core, lo : lo + n, :, rows_at(a, 32), :]

    def to_core(self, g, i, a):
        args = (self.c_send.at[1 + i, g], self.c_recv.at[1 + i, g], self.sib)
        out = remote(self.band(g, a, self.core), self.band(g, a, self.core), *args)
        out.start()
        self.flying["back", g, i] = (out, remote(self.band(g, a, self.core), self.band(g, a, 1 - self.core), *args))

    def gather_first(self, g):
        axes = GROUPS[g][2]
        self.finish(3, g)
        a = self.pos[axes[0]]
        dst = lambda k, a: self.band(g, a, self.core)
        self.exchange(4, g, lambda q: self.band(g, a, self.core), dst, dst, axes[0])
        self.to_core(g, 0, a)

    def gather_core(self, g):
        a = self.pos[GROUPS[g][2][0]]
        for i, (out, back) in enumerate(self.flying[4, g]):
            back.wait_recv()
            self.to_core(g, 1 + i, (a + 3 - i) % 4)

    def end(self, g):
        for i in range(4):
            out, back = self.flying["back", g, i]
            back.wait_recv()

    def drain(self, g):
        for stage in range(5):
            for out, back in self.flying[stage, g]:
                out.wait_send()
        for i in range(4):
            self.flying["back", g, i][0].wait_send()


def ar_scratch():
    n = len(GROUPS)
    bufs = [
        pltpu.VMEM((MATS, 2, TILE, TILE), BF),
        pltpu.VMEM((MATS, 2, TILE, TILE), BF),
        pltpu.VMEM((MATS, 2, TILE, TILE), BF),
        pltpu.VMEM((2, MATS, 2, TILE, TILE), BF),
    ]
    bufs += [pltpu.VMEM((3, g[1], 2, 32, TILE), BF) for g in GROUPS]
    bufs += [pltpu.VMEM((4, g[1], 16, TILE), F32) for g in GROUPS]
    bufs += [pltpu.VMEM((3, g[1], 16, TILE), F32) for g in GROUPS]
    bufs += [pltpu.VMEM((4, g[1], 16, TILE), F32) for g in GROUPS]
    sems = [
        pltpu.SemaphoreType.DMA((5, n)),
        pltpu.SemaphoreType.DMA((5, n)),
        pltpu.SemaphoreType.DMA((5, n, 3)),
        pltpu.SemaphoreType.DMA((5, n, 3)),
    ]
    return bufs, sems


def split_ar(refs):
    n = len(GROUPS)
    bufs = (*refs[:4], refs[4 : 4 + n], refs[4 + n : 4 + 2 * n], refs[4 + 2 * n : 4 + 3 * n], refs[4 + 3 * n : 4 + 4 * n])
    return bufs, refs[4 + 4 * n :]


def body(
    x_in, cot_in, cw_in, cb_in, dw_in, td_in, tu_in, cd_in, cu_in, live_in,
    gi_out, sums_out,
    xs, cext, cw, cb, dw, tiles, vown, send_l, send_r, recv_l, recv_r, big, mask,
    wcat, cwt, ht, xt, ab, feats, gps, gacc, cacc, bacc, gi, cd, cu, live_at,
    load_sem, store_sem, tile_send, tile_recv, pass_send, pass_recv, halo_send, halo_recv, *ar_refs,
):
    b, e, core, pos = place()
    right, left = ((b + 1) % 16, e), ((b + 15) % 16, e)
    sib = (b + 1 - 2 * core, e)
    barrier = pltpu.get_barrier_semaphore()
    greeted = [left, right] + [
        peer(core, pos, {axis: (pos[axis] + k) % 4}) for axis in ("x", "y", "z") for k in (1, 2, 3)
    ]
    for to in greeted:
        pl.semaphore_signal(barrier, inc=1, device_id=to, device_id_type=MESH)
    loads = [
        pltpu.make_async_copy(src, dst, load_sem.at[i])
        for i, (src, dst) in enumerate(
            [
                (live_in, live_at),
                (cd_in, cd),
                (cu_in, cu),
                (td_in, tiles.at[0]),
                (tu_in, tiles.at[1]),
                (x_in, xs),
                (cw_in, cw),
                (cb_in, cb),
                (cot_in, cext.at[:, 2 * TILE : 2 * TILE + ROWS, :]),
                (dw_in, dw),
            ]
        )
    ]
    for load in loads:
        load.start()

    loads[0].wait()
    live = live_at[0]
    reach = lax.broadcasted_iota(jnp.int32, (ROWS, CH), 0)
    mask[...] = jnp.where((reach < live - TILE) | (reach >= ROWS - TILE), 1.0, 0.0).astype(F32)
    for load in loads[1:5]:
        load.wait()
    for way, cols in enumerate((cd, cu)):
        for r in range(NB):
            keep = mask[r * TILE : (r + 1) * TILE, :TILE]
            slots = [tiles[way, r, k].astype(F32) for k in range(4)]
            for o in range(3):
                total = jnp.zeros((TILE, TILE), F32)
                if o == 0:
                    total = total + slots[0]
                if o == 2:
                    total = total + slots[1]
                for k in (2, 3):
                    total = total + jnp.where(cols[r, k] - r == o, 1.0, 0.0).astype(F32) * slots[k]
                total = total * keep
                if r == 0 and o == 0:
                    total = total * jnp.where(b > 0, 1.0, 0.0).astype(F32)
                if r == NB - 1 and o == 2:
                    total = total * jnp.where(b < 15, 1.0, 0.0).astype(F32)
                tile = total.T.astype(BF)
                vown[way, r, o] = tile
                if (r, o) in ((1, 2), (2, 1), (2, 2)):
                    send_r[way, ((1, 2), (2, 1), (2, 2)).index((r, o))] = tile
                if (r, o) in ((0, 0), (0, 1), (1, 0)):
                    send_l[way, ((0, 0), (0, 1), (1, 0)).index((r, o))] = tile

    pl.semaphore_wait(barrier, len(greeted))

    def halo(t):
        return [
            remote(
                cot_in.at[t, TILE:ROWS, :], cext.at[t, 0 : 2 * TILE, :],
                halo_send.at[t, 0], halo_recv.at[t, 0], right,
            ),
            remote(
                cot_in.at[t, 0 : 2 * TILE, :], cext.at[t, 2 * TILE + ROWS : EXT, :],
                halo_send.at[t, 1], halo_recv.at[t, 1], left,
            ),
        ]

    def halo_start(t):
        for copy in halo(t):
            copy.start()

    own = rows_at(pos["z"], 32)
    tile_copies = [
        remote(src.at[:, :, own, :], dst.at[:, :, own, :], tile_send.at[i], tile_recv.at[i], to)
        for i, (src, dst, to) in enumerate([(send_r, recv_l, right), (send_l, recv_r, left)])
    ]
    for copy in tile_copies:
        copy.start()
    halo_start(0)

    for load in loads[5:]:
        load.wait()

    def forward(t):
        pre = dot(xs[t], cw[0]) + dot(xs[t + STEP], cw[1]) + cb[...]
        f = jnp.tanh(pre[:, :CH])
        s = 0.5 * jnp.tanh(0.5 * pre[:, CH:]) + 0.5
        sm = s * mask[...]
        fs = f * sm
        ht[t] = fs.astype(BF).T
        ab[t, :, :CH] = sm * (1.0 - f * f)
        ab[t, :, CH:] = fs * (1.0 - s)

    pl.loop(0, T_OUT)(forward)
    passes = []
    for i, ref in enumerate((recv_l, recv_r)):
        tile_copies[i].wait()
        for k in (1, 2, 3):
            args = (pass_send.at[i, k - 1], pass_recv.at[i, k - 1], peer(core, pos, {"z": (pos["z"] + k) % 4}))
            theirs = rows_at((pos["z"] + 4 - k) % 4, 32)
            out = remote(ref.at[:, :, own, :], ref.at[:, :, own, :], *args)
            out.start()
            passes.append((out, remote(ref.at[:, :, own, :], ref.at[:, :, theirs, :], *args)))
    halo_start(1)
    halo_start(2)

    @pl.loop(0, T_IN)
    def _(t):
        xt[t] = xs[t].T

    for k in range(5):
        wcat[k * CH : (k + 1) * CH, :] = dw[k].T
    for k in range(2):
        cwt[k] = cw[k].T
    gacc[...] = jnp.zeros_like(gacc)
    cacc[...] = jnp.zeros_like(cacc)
    bacc[...] = jnp.zeros_like(bacc)

    for out, back in passes:
        back.wait_recv()
        out.wait_send()

    def v(way, i, k):
        if 0 <= i < NB:
            return vown[way, i, k - i + 1]
        if i < 0:
            return recv_l[way, ((-2, -1), (-1, -1), (-1, 0)).index((i, k))]
        return recv_r[way, ((3, 2), (3, 3), (4, 3)).index((i, k))]

    for j in range(NB):
        for way in range(2):
            for at, i in enumerate(range(j - 2, j + 3)):
                total = jnp.zeros((TILE, TILE), F32)
                for k in range(j - 1, j + 2):
                    if abs(i - k) <= 1:
                        total = total + dot(v(way, k, j), v(way, i, k))
                first = v(way, i, j) if abs(i - j) <= 1 else jnp.zeros((TILE, TILE), BF)
                big[j, way * TILE : (way + 1) * TILE, at * TILE : (at + 1) * TILE] = first
                big[j, (2 + way) * TILE : (3 + way) * TILE, at * TILE : (at + 1) * TILE] = total.astype(BF)

    def diffuse(t):
        for copy in halo(t):
            copy.wait_recv()
        if not isinstance(t, int):
            pl.when(t + 3 < T_OUT)(lambda: halo_start(t + 3))
        feats[:, :CH] = cext[t, 2 * TILE : 2 * TILE + ROWS, :]
        for j in range(NB):
            out = dot(big[j], cext[t, j * TILE : (j + 5) * TILE, :]).astype(BF)
            for at, k in enumerate((1, 3, 2, 4)):
                feats[j * TILE : (j + 1) * TILE, k * CH : (k + 1) * CH] = out[at * TILE : (at + 1) * TILE]
        gacc[...] += dot(ht[t], feats[...])

    def backward(t):
        gh = dot(feats[...], wcat[...])
        ga = gh * ab[t, :, :CH]
        gb = gh * ab[t, :, CH:]
        gp = jnp.concatenate([ga, gb], axis=1).astype(BF)
        gps[t] = gp
        cacc[...] += dot(jnp.concatenate([xt[t], xt[t + STEP]], axis=0), gp).reshape(2, CH, 2 * CH)
        bacc[...] += jnp.sum(gp.astype(F32).reshape(ROWS // 8, 8, 2 * CH), axis=0)

    @pl.loop(0, T_OUT - 1)
    def _(t):
        diffuse(t)
        backward(t)

    def half_of(m, c, half):
        if m < 5:
            return gacc[rows_at(half, TILE), m * CH + c * TILE : m * CH + (c + 1) * TILE]
        if m < 9:
            at = ((m - 5) % 2) * CH + c * TILE
            return cacc[(m - 5) // 2, rows_at(half, TILE), at : at + TILE]
        line = jnp.sum(bacc[...], axis=0, keepdims=True)
        row = lax.broadcasted_iota(jnp.int32, (16, TILE), 0)
        bias = jnp.zeros((16, TILE), F32)
        for i in range(4):
            part = jnp.broadcast_to(line[:, i * TILE : (i + 1) * TILE], (16, TILE))
            bias = bias + jnp.where(row == i, part, 0.0)
        return jnp.broadcast_to(bias[None], (TILE // 16, 16, TILE)).reshape(TILE, TILE)

    stores = []

    def inputs_grad(t):
        total = jnp.zeros((ROWS, CH), F32)
        if t < T_OUT:
            total = total + dot(gps[t], cwt[0])
        if t >= STEP:
            own_cot = cext[t - STEP, 2 * TILE : 2 * TILE + ROWS, :].astype(F32)
            total = total + dot(gps[t - STEP], cwt[1]) + own_cot * mask[...]
        gi[t] = total.astype(BF)
        store = pltpu.make_async_copy(gi.at[t], gi_out.at[t], store_sem.at[t])
        store.start()
        stores.append(store)

    bufs, sems = split_ar(ar_refs)
    reduce = AllReduce(half_of, core, pos, sib, bufs, sems)
    groups = range(len(GROUPS))
    diffuse(T_OUT - 1)
    reduce.core_send(0)
    backward(T_OUT - 1)
    for g in groups[1:]:
        reduce.core_send(g)
    for stage, steps in (
        (reduce.scatter_first, (0, 1)),
        (reduce.scatter_second, (2, 3)),
        (reduce.sum_third, (4, 5)),
        (reduce.gather_second, (6, 7)),
        (reduce.gather_first, ()),
        (reduce.gather_core, ()),
        (reduce.end, ()),
    ):
        for g in groups:
            stage(g)
        for t in steps:
            inputs_grad(t)
    last = pltpu.make_async_copy(bufs[3], sums_out, store_sem.at[T_IN])
    last.start()
    for t in range(T_OUT):
        for copy in halo(t):
            copy.wait_send()
    for g in groups:
        reduce.drain(g)
    for store in stores:
        store.wait()
    last.wait()


def unpack(scale, gi_in, sums_in, gi_out, gc_out, gb_out, gd_out, gi, sums, gc, gd, sem):
    first = pltpu.make_async_copy(sums_in, sums, sem.at[0, T_IN])
    ins = [pltpu.make_async_copy(gi_in.at[t], gi.at[t], sem.at[0, t]) for t in range(T_IN)]
    outs = [pltpu.make_async_copy(gi.at[t], gi_out.at[t], sem.at[1, t]) for t in range(T_IN)]
    first.start()
    for copy in ins:
        copy.start()
    first.wait()
    for copy, out in zip(ins, outs):
        copy.wait()
        out.start()
    for m in range(9):
        for h in range(2):
            for c in range(2):
                rows = slice(h * TILE, (h + 1) * TILE)
                part = sums[h, m, c].astype(F32) * scale
                if m < 5:
                    gd[m, rows, c * TILE : (c + 1) * TILE] = part
                else:
                    at = ((m - 5) % 2) * CH + c * TILE
                    gc[(m - 5) // 2, rows, at : at + TILE] = part
        if m == 4:
            outs.append(pltpu.make_async_copy(gd, gd_out, sem.at[1, T_IN]))
            outs[-1].start()
    outs.append(pltpu.make_async_copy(gc, gc_out, sem.at[1, T_IN + 1]))
    outs[-1].start()
    bias = sums[0, 9, 0, 0:16, :].astype(F32) * scale
    for i in range(4):
        gb_out[:, i * TILE : (i + 1) * TILE] = bias[i : i + 1]
    for out in outs:
        out.wait()


def on_device(x, cot, cw, cb, dw, td, tu, cd, cu, live):
    scale = float(8 * T_OUT * 6144) ** (-0.5)
    bufs, sems = ar_scratch()
    anywhere = pl.BlockSpec(memory_space=pl.ANY)
    vmem = pl.BlockSpec(memory_space=pltpu.VMEM)
    gi, sums = pl.pallas_call(
        body,
        out_shape=(
            jax.ShapeDtypeStruct((T_IN, ROWS, CH), BF),
            jax.ShapeDtypeStruct((2, MATS, 2, TILE, TILE), BF),
        ),
        in_specs=[anywhere] * 10,
        out_specs=(anywhere,) * 2,
        scratch_shapes=[
            pltpu.VMEM((T_IN, ROWS, CH), BF),
            pltpu.VMEM((T_OUT, EXT, CH), BF),
            pltpu.VMEM((2, CH, 2 * CH), BF),
            pltpu.VMEM((1, 2 * CH), F32),
            pltpu.VMEM((5, CH, CH), BF),
            pltpu.VMEM((2, NB, 4, TILE, TILE), BF),
            pltpu.VMEM((2, NB, 3, TILE, TILE), BF),
            pltpu.VMEM((2, 3, TILE, TILE), BF),
            pltpu.VMEM((2, 3, TILE, TILE), BF),
            pltpu.VMEM((2, 3, TILE, TILE), BF),
            pltpu.VMEM((2, 3, TILE, TILE), BF),
            pltpu.VMEM((NB, 4 * TILE, 5 * TILE), BF),
            pltpu.VMEM((ROWS, CH), F32),
            pltpu.VMEM((5 * CH, CH), BF),
            pltpu.VMEM((2, 2 * CH, CH), BF),
            pltpu.VMEM((T_OUT, CH, ROWS), BF),
            pltpu.VMEM((T_IN, CH, ROWS), BF),
            pltpu.VMEM((T_OUT, ROWS, 2 * CH), F32),
            pltpu.VMEM((ROWS, 5 * CH), BF),
            pltpu.VMEM((T_OUT, ROWS, 2 * CH), BF),
            pltpu.VMEM((CH, 5 * CH), F32),
            pltpu.VMEM((2, CH, 2 * CH), F32),
            pltpu.VMEM((8, 2 * CH), F32),
            pltpu.VMEM((T_IN, ROWS, CH), BF),
            pltpu.SMEM((NB, 4), jnp.int32),
            pltpu.SMEM((NB, 4), jnp.int32),
            pltpu.SMEM((1,), jnp.int32),
            pltpu.SemaphoreType.DMA((10,)),
            pltpu.SemaphoreType.DMA((T_IN + 1,)),
            pltpu.SemaphoreType.DMA((2,)),
            pltpu.SemaphoreType.DMA((2,)),
            pltpu.SemaphoreType.DMA((2, 3)),
            pltpu.SemaphoreType.DMA((2, 3)),
            pltpu.SemaphoreType.DMA((T_OUT, 2)),
            pltpu.SemaphoreType.DMA((T_OUT, 2)),
            *bufs,
            *sems,
        ],
        compiler_params=pltpu.CompilerParams(
            collective_id=0, has_side_effects=True, vmem_limit_bytes=61 << 20
        ),
    )(x[0], cot[0], cw, cb.reshape(1, -1), dw, td, tu, cd, cu, live)
    gi, gc, gb, gd = pl.pallas_call(
        functools.partial(unpack, scale),
        out_shape=(
            jax.ShapeDtypeStruct((T_IN, ROWS, CH), BF),
            jax.ShapeDtypeStruct((2, CH, 2 * CH), F32),
            jax.ShapeDtypeStruct((1, 2 * CH), F32),
            jax.ShapeDtypeStruct((5, CH, CH), F32),
        ),
        in_specs=[anywhere] * 2,
        out_specs=(anywhere, anywhere, vmem, anywhere),
        scratch_shapes=[
            pltpu.VMEM((T_IN, ROWS, CH), BF),
            pltpu.VMEM((2, MATS, 2, TILE, TILE), BF),
            pltpu.VMEM((2, CH, 2 * CH), F32),
            pltpu.VMEM((5, CH, CH), F32),
            pltpu.SemaphoreType.DMA((2, T_IN + 2)),
        ],
        compiler_params=pltpu.CompilerParams(vmem_limit_bytes=61 << 20),
    )(gi, sums)
    return gi[None], gc, gb.reshape(-1), gd


def solution(mesh):
    return jax.shard_map(
        on_device,
        mesh=mesh,
        in_specs=(
            P("event", None, "basin", None),
            P("event", None, "basin", None),
            P(),
            P(),
            P(),
            P("basin", None, None, None),
            P("basin", None, None, None),
            P("basin", None),
            P("basin", None),
            P("basin"),
        ),
        out_specs=(P("event", None, "basin", None), P(), P(), P()),
        check_vma=False,
    )
```

time: 74.1 us -> 65 us (0.88)
  local copies, waits for them, and re-layouts: 6.75 us -> 0 us
  Pallas kernels: 65.8 us -> 63.6 us
    unnamed x7 -> x0, local copies, waits for them, and re-layouts: 5.49 us -> none
    pallas_call x1 -> x2, Pallas kernels: 65.8 us -> 63.6 us  [the longest x1 59.6 us: on_device(): pl.pallas_call(body, out_shape=(jax.ShapeDtypeStruct((T_IN, ROWS, CH), BF...]
    reshape x1 -> x0, local copies, waits for them, and re-layouts: 1.25 us -> none  [on_device(): return (gi[None], gc, gb[0:4].reshape(-1), gd)]
where the time goes in v1:
time: 65 us; the launch traced here: 64.9 us
  Pallas kernels  63.6 us (98%)
  between operations  1.29 us (2%)
    pallas_call x1, Pallas kernels, on_device(): pl.pallas_call(body, out_shape=(jax.ShapeDtypeStruct((T_IN, ROWS, CH), BF...  59.6 us
    pallas_call x1, Pallas kernels, on_device(): pl.pallas_call(functools.partial(unpack, scale), out_shape=(jax.ShapeDtyp...  3.99 us

profile of v1, /device:TPU:1, one launch (start us, length us, event | category | flops | bytes accessed | tf_op | source)
XLA Modules:
  0.0 64.9 jit_solution(14693994866915421008)
XLA Ops:
  1.3 59.6 %shard_map.129 = (bf16[8,384,256]{2,1,0:T(8,128)(2,1)}, bf16[2,10,2,128,128]{4,3,2,1,0:T(8,128)(2,1)}) custom-call(bf16[8,384,256]{2,1,0:T(8,128)(2,1)} %bitcast.5, bf16[6,384,256]{2,1,0:T(8,128)(2,1)} %bitcast.6, bf16[2,256,512]{2,1,0:T(8,128)(2,1)} %cw_in.1, f32[1,512]{1,0:T(1,128)} %bitcast.7, bf16[5,256,256]{2,1,0:T(8,128)(2,1)} %dw_in.1, ...), custom_call_target="tpu_custom_call" | custom-call | tf_op jit(solution)/shard_map/pallas_call | solution.py:471
  60.9 4.0 %shard_map.130 = (bf16[8,384,256]{2,1,0:T(8,128)(2,1)}, f32[2,256,512]{2,1,0:T(8,128)}, f32[1,512]{1,0:T(1,128)}, f32[5,256,256]{2,1,0:T(8,128)}) custom-call(bf16[8,384,256]{2,1,0:T(8,128)(2,1)} %get-tuple-element.10.gi_in, bf16[2,10,2,128,128]{4,3,2,1,0:T(8,128)(2,1)} %get-tuple-element.11.sums_in), custom_call_target="tpu_custom_call" | custom-call | tf_op jit(solution)/shard_map/pallas_call | solution.py:522
